TPU v7x, 32 devices: a whole 2x2x4 slice. The times are simulated.
32 devices in a mesh: pts: 16 (over z, y, core), freq: 2 (over x).
Axes of the slice: x: 2, y: 2, z: 4, core: 2. Of those that a mesh axis runs over, the one named last changes fastest.
Arguments:
- snapshots: float32 [2112, 12288], P(None, ('pts', 'freq')), may hold values from -6 to 6
- weight: float32 [12288], P('pts'), may hold values from 0.1 to 10
- start_vec: float32 [64, 2, 32], replicated, may hold values from -6 to 6
Outputs:
- gram_mine: float32 [64, 2, 32, 32], P('freq')
- modes: float32 [64, 2, 12288], P('freq', None, 'pts')
All inputs are finite; a program needn't handle non-finite values.
Results may differ from a plain program's by a relative error of at most 0.0003.
Values sent between devices are 32-bit elements; how exact they have to be, the bound alone decides.
No kernel may reach another device: no remote copies, remote signals or barrier semaphores. Data moves between devices by JAX's collectives and lax.ppermute only.
A program may use at most 64 MiB of HBM per device.

v0:
```python
import functools
import math

import jax
import jax.numpy as jnp
import numpy as np
from jax import lax
from jax.experimental import pallas as pl
from jax.experimental.pallas import tpu as pltpu
from jax.sharding import PartitionSpec as P

NFFT = 128
HALF = NFFT // 2
NF = 64
NB = 32
LANES = 128
PACK = 4
VMEM_LIMIT = 51 * 1024 * 1024
SMALL_LIMIT = 8 * 1024 * 1024
MODES_LIMIT = 24 * 1024 * 1024
UNPACK_LIMIT = 53 * 1024 * 1024
VMEM = pl.BlockSpec(memory_space=pltpu.VMEM)


def dft_values():
    times = np.arange(NFFT)
    freqs = np.arange(NF)
    phases = (freqs[:, None] * times[None, :] % NFFT) * (2.0 * math.pi / NFFT)
    window = 0.5 - 0.5 * np.cos(times * (2.0 * math.pi / NFFT))
    weighted = window / np.sqrt(np.sum(window * window))
    return np.cos(phases) * weighted, -np.sin(phases) * weighted


def split_table(table):
    high = table.astype(jnp.bfloat16)
    low = (table - high.astype(np.float64)).astype(jnp.bfloat16)
    return high, low


def window_leaks():
    real, _ = dft_values()
    return [float(np.sum(real[k])) for k in range(2)]


def mode_tables():
    real, imag = dft_values()
    order = np.arange(NF).reshape(NF // PACK, PACK).T
    real, imag = real[order], imag[order]
    first = np.stack([real, imag], axis=1).reshape(2 * NF, NFFT)
    second = np.stack([-imag, real], axis=1).reshape(2 * NF, NFFT)
    return np.stack([first, second]).astype(np.float32)


def cosine_of_turns(count):
    folded = jnp.minimum(count, NFFT - count)
    angle = (NFFT // 4 - folded).astype(jnp.float32) * (2.0 * math.pi / NFFT)
    square = angle * angle
    series = 1.0
    for n in (10, 8, 6, 4, 2):
        series = 1.0 - square * series * (1.0 / (n * (n + 1)))
    return angle * series


def fill_dft(dft_ref):
    row = lax.broadcasted_iota(jnp.int32, (2 * NF, NFFT), 0)
    time = lax.broadcasted_iota(jnp.int32, (2 * NF, NFFT), 1)
    quarter = jnp.where(row < NF, 0, NFFT // 4)
    wave = cosine_of_turns((row % NF * time + quarter) % NFFT)
    window = 0.5 - 0.5 * np.cos(np.arange(NFFT) * (2.0 * math.pi / NFFT))
    norm = float(np.sqrt(np.sum(window * window)))
    high, low = split(wave * ((0.5 - 0.5 * cosine_of_turns(time)) / norm))
    dft_ref[pl.ds(0, 2 * NF), pl.ds(0, NFFT)] = high
    dft_ref[pl.ds(0, 2 * NF), pl.ds(NFFT, NFFT)] = high
    dft_ref[pl.ds(2 * NF, 2 * NF), pl.ds(0, NFFT)] = low
    dft_ref[pl.ds(2 * NF, 2 * NF), pl.ds(NFFT, NFFT)] = jnp.zeros((2 * NF, NFFT), jnp.bfloat16)


def spread_start(start_ref, spread_ref):
    row = lax.broadcasted_iota(jnp.int32, (NF, LANES), 0)
    lane = lax.broadcasted_iota(jnp.int32, (NF, LANES), 1)
    start = start_ref[pl.ds(0, 2 * NB), pl.ds(0, NF)]
    for g in range(NF // PACK):
        pick = (row == PACK * g + lane // NB).astype(jnp.float32)
        spread_ref[g] = jnp.dot(
            start,
            pick,
            precision=lax.Precision.HIGHEST,
            preferred_element_type=jnp.float32,
        )


def split(value):
    high = value.astype(jnp.bfloat16)
    low = (value - high.astype(jnp.float32)).astype(jnp.bfloat16)
    return high, low


def load_weights(w_ref, col_tiles):
    first = lax.axis_index("freq") * col_tiles
    return jnp.concatenate([w_ref[pl.ds(first + c, 1), :] for c in range(col_tiles)], axis=1)


def flip_groups(groups, flipped):
    turned = flipped.T
    lane = lax.broadcasted_iota(jnp.int32, (NB, LANES), 1)
    out = []
    for g in range(PACK):
        total = groups[g]
        for q in range(PACK):
            block = turned[q * NB : (q + 1) * NB]
            if q != g:
                block = pltpu.roll(block, ((q - g) % PACK) * NB, 1)
            total = total + jnp.where(lane // NB == q, block, 0.0)
        out.append(total)
    return out


TILE = 8


def turn_tiles(tiles):
    row = lax.broadcasted_iota(jnp.int32, (TILE, LANES), 0)
    step = TILE // 2
    while step:
        keep = row % (2 * step) < step
        turned = list(tiles)
        for i in range(TILE):
            if i % (2 * step) < step:
                low, high = tiles[i], tiles[i + step]
                turned[i] = jnp.where(keep, low, pltpu.roll(high, step, 0))
                turned[i + step] = jnp.where(keep, pltpu.roll(low, TILE - step, 0), high)
        tiles = turned
        step //= 2
    return tiles


def core_bit():
    return lax.rem(lax.axis_index("pts"), 2)


def y_bit():
    return lax.rem(lax.div(lax.axis_index("pts"), 2), 2)


RESP_ROWS = 2 * NF // PACK


def give_half(value_ref, bit, keep_ref, send_ref):
    half = keep_ref.shape[0] - RESP_ROWS
    keep_ref[pl.ds(0, half), :] = value_ref[pl.ds(bit * half, half), :]
    send_ref[pl.ds(0, half), :] = value_ref[pl.ds((1 - bit) * half, half), :]
    resp = value_ref[pl.ds(2 * half, RESP_ROWS), :]
    keep_ref[pl.ds(half, RESP_ROWS), :] = resp
    send_ref[pl.ds(half, RESP_ROWS), :] = resp


def gram_kernel(
    total_rows,
    places,
    by_core,
    x_hbm,
    aux_ref,
    keep_ref,
    send_ref,
    high_ref,
    rest_ref,
    low_hbm,
    x_ref,
    dft_ref,
    low_ref,
    block_even,
    block_odd,
    spec_ref,
    z_even,
    z_odd,
    real_ref,
    imag_ref,
    spread_ref,
    pack_ref,
    in_sems,
    out_sem,
):
    times, cols = x_ref.shape
    col_tiles = cols // LANES
    block_refs = (block_even, block_odd)
    cuts = [0] + [(first + TILE + 1) * HALF for first in range(0, NB, TILE)]

    def fetches(i):
        middle = (cuts[i] + cuts[i + 1]) // (2 * HALF) * HALF
        for n, (first, last) in enumerate(((cuts[i], middle), (middle, cuts[i + 1]))):
            rows = pl.ds(first, last - first)
            yield pltpu.make_async_copy(x_hbm.at[rows], x_ref.at[rows], in_sems.at[2 * i + n])

    for i in range(len(cuts) - 1):
        for fetch in fetches(i):
            fetch.start()
    fill_dft(dft_ref)
    spread_start(aux_ref, spread_ref)
    weights = load_weights(aux_ref.at[pl.ds(2 * NB, aux_ref.shape[0] - 2 * NB)], col_tiles)
    scale = jnp.sqrt(weights / (2.0 * total_rows))
    for fetch in fetches(0):
        fetch.wait()
    first_mean = jnp.mean(x_ref[pl.ds(0, NFFT), :], axis=0, keepdims=True)

    def center(i, acc):
        def step(h, acc):
            rows = pl.ds(pl.multiple_of(h * HALF, HALF), HALF)
            value = x_ref[rows, :] - first_mean
            high, low = split(value * scale)
            high_ref[rows, :] = high
            low_ref[rows, :] = low
            return acc + value

        return lax.fori_loop(cuts[i] // HALF, cuts[i + 1] // HALF, step, acc, unroll=True)

    def transform(first):
        for i in range(TILE // 2):
            blocks = []
            for s in range(2):
                rows = pl.ds((first + 2 * i + s) * HALF, NFFT)
                blocks.append(jnp.concatenate([high_ref[rows, :], low_ref[rows, :]], axis=0))
            both = jnp.dot(
                dft_ref[...], jnp.concatenate(blocks, axis=1), preferred_element_type=jnp.float32
            )
            spectrum = both[: 2 * NF] + both[2 * NF :]
            for s in range(2):
                block_refs[first // TILE % 2][2 * i + s] = spectrum[:, s * cols : (s + 1) * cols]

    def arrange(first):
        block_ref = block_refs[first // TILE % 2]
        for c in range(col_tiles):
            lanes = pl.ds(c * LANES, LANES)
            for o in range(2 * NF // TILE):
                rows = pl.ds(o * TILE, TILE)
                tiles = turn_tiles([block_ref[b, rows, lanes] for b in range(TILE)])
                for k in range(TILE):
                    spec_ref[c, o * TILE + k, pl.ds(first, TILE), :] = tiles[k]

    acc = center(0, jnp.zeros((HALF, cols), jnp.float32))
    transform(0)
    for first in range(0, NB, TILE):
        if first + TILE < NB:
            for fetch in fetches(first // TILE + 1):
                fetch.wait()
            acc = center(first // TILE + 1, acc)
            transform(first + TILE)
        arrange(first)
    pad = high_ref.shape[0] - times
    if pad:
        high_ref[pl.ds(times, pad), :] = jnp.zeros((pad, cols), jnp.bfloat16)
        low_ref[pl.ds(times, pad), :] = jnp.zeros((pad, cols), jnp.bfloat16)
    save_low = pltpu.make_async_copy(low_ref, low_hbm, out_sem)
    save_low.start()
    rest = jnp.sum(acc, axis=0, keepdims=True) / times * scale
    rest_ref[...] = jnp.broadcast_to(rest, rest_ref.shape)
    for k, leak in enumerate(window_leaks()):
        for c in range(col_tiles):
            part = rest[:, c * LANES : (c + 1) * LANES]
            spec_ref[c, k] = spec_ref[c, k] - leak * part

    row = lax.broadcasted_iota(jnp.int32, (NB, LANES), 0)
    lane = lax.broadcasted_iota(jnp.int32, (NB, LANES), 1)
    upper = row <= lane % NB
    octets = NF // 8

    def prepare(z_ref, octet, half):
        for part in range(2):
            for q in range(PACK):
                own = pl.ds(part * LANES + q * NB, NB)
                for c in range(col_tiles):
                    value = spec_ref[c, NF * part + TILE * octet + PACK * half + q]
                    high = value.astype(jnp.bfloat16)
                    low = (2.0 * (value - high.astype(jnp.float32))).astype(jnp.bfloat16)
                    z_ref[own, pl.ds(c * LANES, LANES)] = high
                    z_ref[own, pl.ds(cols + c * LANES, LANES)] = low

    def correlate(z_ref, group):
        high = z_ref[:, pl.ds(0, cols)]
        product = lax.dot_general(
            jnp.concatenate([high, high], axis=1),
            z_ref[...],
            (((1,), (1,)), ((), ())),
            preferred_element_type=jnp.float32,
        )
        gram_real = jnp.zeros((NB, LANES), jnp.float32)
        gram_imag = jnp.zeros((NB, LANES), jnp.float32)
        for q in range(PACK):
            mine = lane // NB == q
            real = product[q * NB : (q + 1) * NB]
            imag = product[LANES + q * NB : LANES + (q + 1) * NB]
            gram_real = jnp.where(mine, real[:, :LANES] + imag[:, LANES:], gram_real)
            gram_imag = jnp.where(mine, real[:, LANES:] - imag[:, :LANES], gram_imag)
        real_ref[group] = gram_real
        imag_ref[group] = gram_imag

    left = lane[: NB // 2] < LANES // 2
    half = NB // 2
    resp_real = []
    resp_imag = []

    def finish_quad(quad):
        own = pl.ds(quad * PACK, PACK)
        reals = [real_ref[quad * PACK + g] for g in range(PACK)]
        imags = [imag_ref[quad * PACK + g] for g in range(PACK)]
        reals = flip_groups(reals, real_ref[own].reshape(PACK * NB, LANES))
        imags = flip_groups(imags, -imag_ref[own].reshape(PACK * NB, LANES))
        for g, (real, imag) in enumerate(zip(reals, imags)):
            group = quad * PACK + g
            start_real = spread_ref[group, pl.ds(0, NB), :]
            start_imag = spread_ref[group, pl.ds(NB, NB), :]
            resp_real.append(
                jnp.sum(real * start_real + imag * start_imag, axis=0, keepdims=True)
            )
            resp_imag.append(
                jnp.sum(real * start_imag - imag * start_real, axis=0, keepdims=True)
            )
            packed = jnp.where(upper, real, imag)
            top = packed[:half]
            bottom = packed[half:]
            even = jnp.where(left, top, pltpu.roll(bottom, LANES // 2, 1))
            odd = jnp.where(left, pltpu.roll(top, LANES // 2, 1), bottom)
            pack_ref[pl.ds(places[2 * group] * half, half), :] = even
            pack_ref[pl.ds(places[2 * group + 1] * half, half), :] = odd

    z_refs = (z_even, z_odd)
    groups = NF // PACK
    prepare(z_even, 0, 0)
    for group in range(groups):
        if group + 1 < groups:
            prepare(z_refs[(group + 1) % 2], (group + 1) // 2, (group + 1) % 2)
        correlate(z_refs[group % 2], group)
        if group % PACK == PACK - 1:
            finish_quad(group // PACK)
    resp = jnp.concatenate(resp_real + resp_imag, axis=0)
    pack_ref[pl.ds(NF // 2 * half, RESP_ROWS), :] = resp
    give_half(pack_ref, core_bit() if by_core else 0, keep_ref, send_ref)
    save_low.wait()


def gram_parts(snapshots, weight_rows, start_vec, total_rows, places, by_core):
    times, cols = snapshots.shape
    start = jnp.transpose(start_vec, (1, 2, 0)).reshape(2 * NB, NF)
    start = jnp.pad(start, ((0, 0), (0, LANES - NF)))
    aux = jnp.concatenate([start, weight_rows], axis=0)
    any_space = pl.BlockSpec(memory_space=pl.ANY)
    saved = jax.ShapeDtypeStruct((-(-times // LANES) * LANES, cols), jnp.bfloat16)
    half = floats(NF // 4 * NB // 2 + RESP_ROWS, LANES)
    return pl.pallas_call(
        functools.partial(gram_kernel, total_rows, places, by_core),
        out_shape=(half, half, saved, floats(8, cols), saved),
        in_specs=[any_space, VMEM],
        out_specs=(VMEM, VMEM, VMEM, VMEM, any_space),
        scratch_shapes=[
            pltpu.VMEM((times, cols), jnp.float32),
            pltpu.VMEM((4 * NF, 2 * NFFT), jnp.bfloat16),
            pltpu.VMEM(saved.shape, jnp.bfloat16),
            pltpu.VMEM((TILE, 2 * NF, cols), jnp.float32),
            pltpu.VMEM((TILE, 2 * NF, cols), jnp.float32),
            pltpu.VMEM((cols // LANES, 2 * NF, NB, LANES), jnp.float32),
            pltpu.VMEM((2 * LANES, 2 * cols), jnp.bfloat16),
            pltpu.VMEM((2 * LANES, 2 * cols), jnp.bfloat16),
            pltpu.VMEM((NF // PACK, NB, LANES), jnp.float32),
            pltpu.VMEM((NF // PACK, NB, LANES), jnp.float32),
            pltpu.VMEM((NF // PACK, 2 * NB, LANES), jnp.float32),
            pltpu.VMEM((NF // 2 * NB // 2 + RESP_ROWS, LANES), jnp.float32),
            pltpu.SemaphoreType.DMA((2 * NB // TILE,)),
            pltpu.SemaphoreType.DMA(()),
        ],
        compiler_params=pltpu.CompilerParams(vmem_limit_bytes=VMEM_LIMIT),
        cost_estimate=pl.CostEstimate(
            flops=5_000_000_000, bytes_accessed=8_000_000, transcendentals=0
        ),
        name="gram_parts",
    )(snapshots, aux)


def pair_square(even, odd):
    left = lax.broadcasted_iota(jnp.int32, (NB // 2, LANES), 1) < LANES // 2
    top = jnp.where(left, even, pltpu.roll(odd, LANES // 2, 1))
    bottom = jnp.where(left, pltpu.roll(even, LANES // 2, 1), odd)
    return jnp.concatenate([top, bottom], axis=0)


def hermitian(squares):
    row = lax.broadcasted_iota(jnp.int32, (NB, LANES), 0)
    col = lax.broadcasted_iota(jnp.int32, (NB, LANES), 1) % NB
    zero = jnp.zeros((NB, LANES), jnp.float32)
    full = squares + [zero] * (PACK - len(squares))
    turned = flip_groups([zero] * PACK, jnp.concatenate(full, axis=0))
    for square, flipped in zip(squares, turned):
        real = jnp.where(row <= col, square, flipped)
        imag = jnp.where(row > col, square, jnp.where(row < col, -flipped, 0.0))
        yield real, imag


def small_call(kernel, name, out_shape, scratch_shapes=(), limit=SMALL_LIMIT):
    def call(*args):
        return pl.pallas_call(
            kernel,
            out_shape=out_shape,
            in_specs=[VMEM] * len(args),
            out_specs=VMEM if isinstance(out_shape, jax.ShapeDtypeStruct) else (VMEM,) * len(out_shape),
            scratch_shapes=list(scratch_shapes),
            compiler_params=pltpu.CompilerParams(vmem_limit_bytes=limit),
            name=name,
        )(*args)

    return call


def floats(*shape):
    return jax.ShapeDtypeStruct(shape, jnp.float32)


def add_core_kernel(kept_ref, got_ref, out_ref):
    quarter = out_ref.shape[1] - RESP_ROWS
    tail = pl.ds(4 * quarter, RESP_ROWS)
    resp = kept_ref[tail, :] + got_ref[tail, :]
    for m in range(4):
        rows = pl.ds(m * quarter, quarter)
        out_ref[m, pl.ds(0, quarter), :] = kept_ref[rows, :] + got_ref[rows, :]
        out_ref[m, pl.ds(quarter, RESP_ROWS), :] = resp


def add_core(kept, got):
    quarter = (kept.shape[0] - RESP_ROWS) // 4
    return small_call(add_core_kernel, "add_core", floats(4, quarter + RESP_ROWS, LANES))(kept, got)


def add_near_kernel(parts_ref, out_ref):
    out_ref[...] = (parts_ref[0] + parts_ref[1]) + (parts_ref[2] + parts_ref[3])


def add_kernel(kept_ref, got_ref, out_ref):
    out_ref[...] = kept_ref[...] + got_ref[...]


def add(name, kept, got):
    return small_call(add_kernel, name, floats(*kept.shape))(kept, got)


def finish_kernel(kept_ref, got_ref, packed_ref, resp_ref):
    rows = packed_ref.shape[0]
    packed_ref[...] = kept_ref[pl.ds(0, rows), :] + got_ref[pl.ds(0, rows), :]
    tail = pl.ds(rows, RESP_ROWS)
    resp = kept_ref[tail, :] + got_ref[tail, :]
    real = resp[: RESP_ROWS // 2]
    imag = resp[RESP_ROWS // 2 :]
    power = real * real + imag * imag
    lane = lax.broadcasted_iota(jnp.int32, power.shape, 1)
    mean = jnp.zeros(power.shape, jnp.float32)
    for q in range(PACK):
        mine = lane // NB == q
        part = jnp.sum(jnp.where(mine, power, 0.0), axis=1, keepdims=True) / NB
        mean = jnp.where(mine, part, mean)
    scaling = 1.0 / jnp.sqrt(mean + 1e-06)
    resp_ref[pl.ds(0, RESP_ROWS // 2), :] = real * scaling
    resp_ref[pl.ds(RESP_ROWS // 2, RESP_ROWS // 2), :] = imag * scaling


def finish(kept, got):
    rows = kept.shape[0] - RESP_ROWS
    return small_call(finish_kernel, "finish", (floats(rows, LANES), floats(RESP_ROWS, LANES)))(
        kept, got
    )


def join_y_kernel(own_ref, got_ref, packed_ref):
    rows = own_ref.shape[0]
    for m, ref in enumerate((own_ref, got_ref)):
        packed_ref[pl.ds((y_bit() ^ m) * rows, rows), :] = ref[...]


def unpack_kernel(part_index, *refs):
    part_ref, out_hbm, full_ref, sem = refs[-4:]
    half = NB // 2
    count = part_ref.shape[0] // half
    for first in range(0, count, 2 * PACK):
        last = min(first + 2 * PACK, count)
        pairs = [part_ref[pl.ds(i * half, half), :] for i in range(first, last)]
        squares = [pair_square(*pairs[i : i + 2]) for i in range(0, len(pairs), 2)]
        for g, both in enumerate(hermitian(squares)):
            for q in range(PACK):
                freq = 2 * first + PACK * g + q
                for c in range(2):
                    full_ref[freq, c] = both[c][:, q * NB : (q + 1) * NB]
    start = 0 if part_index is None else (core_bit() ^ part_index) * 2 * count
    copy = pltpu.make_async_copy(full_ref, out_hbm.at[pl.ds(start, 2 * count)], sem)
    copy.start()
    copy.wait()


def unpack_gram(part, part_index=None, done=None):
    count = part.shape[0] * 4 // NB
    total = count if part_index is None else 2 * count
    any_space = pl.BlockSpec(memory_space=pl.ANY)
    before = () if done is None else (done,)
    return pl.pallas_call(
        functools.partial(unpack_kernel, part_index),
        out_shape=floats(total, 2, NB, NB),
        in_specs=[any_space] * len(before) + [VMEM],
        out_specs=any_space,
        scratch_shapes=[
            pltpu.VMEM((count, 2, NB, NB), jnp.float32),
            pltpu.SemaphoreType.DMA(()),
        ],
        input_output_aliases={0: 0} if before else {},
        compiler_params=pltpu.CompilerParams(vmem_limit_bytes=UNPACK_LIMIT),
        name="unpack_own" if part_index == 0 else "unpack_other",
    )(*before, part)


def hand_on_kernel(low_hbm, after_ref, out_ref, token_ref, sem):
    copy = pltpu.make_async_copy(low_hbm, out_ref, sem)
    copy.start()
    token_ref[...] = after_ref[pl.ds(0, TILE), :]
    copy.wait()


def hand_on(low, after):
    return pl.pallas_call(
        hand_on_kernel,
        out_shape=(jax.ShapeDtypeStruct(low.shape, low.dtype), floats(TILE, LANES)),
        in_specs=[pl.BlockSpec(memory_space=pl.ANY), VMEM],
        out_specs=(VMEM, VMEM),
        scratch_shapes=[pltpu.SemaphoreType.DMA(())],
        compiler_params=pltpu.CompilerParams(vmem_limit_bytes=SMALL_LIMIT),
        name="hand_on",
    )(low, after)


def modes_kernel(
    total_rows,
    slot,
    high_ref,
    low_ref,
    rest_ref,
    w_ref,
    table_ref,
    resp_ref,
    out_ref,
    a_ref,
):
    cols = high_ref.shape[1]
    padded = high_ref.shape[0]
    all_groups = RESP_ROWS // 2
    groups = all_groups if slot is None else all_groups // 2
    start = 0 if slot is None else (lax.axis_index("freq") ^ slot) * groups
    count = 2 * groups
    total = PACK * count
    leaks = window_leaks()
    corrections = []
    row = lax.broadcasted_iota(jnp.int32, (count, 1), 0)
    lane = lax.broadcasted_iota(jnp.int32, (count, LANES), 1)
    left = lane < HALF
    parts = [pl.ds(part * all_groups + start, groups) for part in range(2)]
    resp_all = jnp.concatenate([resp_ref[rows, :] for rows in parts], axis=0)
    for q in range(PACK):
        resp = pltpu.roll(resp_all, LANES - q * NB, 1) if q else resp_all
        if q < len(leaks):
            sums = jnp.sum(jnp.where(lane < NB, resp, 0.0), axis=1, keepdims=True) * leaks[q]
            sums = jnp.where(row % groups + start == 0, sums, 0.0)
            corrections.append(sums * rest_ref[pl.ds(0, 1), :])
        else:
            corrections.append(jnp.zeros((count, cols), jnp.float32))
        real = jnp.concatenate([resp[:groups]] * 2, axis=0)
        imag = jnp.concatenate([resp[groups:]] * 2, axis=0)
        tables = []
        for kind in range(2):
            pieces = [
                table_ref[kind, pl.ds(q * RESP_ROWS + part * all_groups + start, groups), :]
                for part in range(2)
            ]
            tables.append(jnp.concatenate(pieces, axis=0))
        first, second = tables
        first_turned = pltpu.roll(first, HALF, 1)
        second_turned = pltpu.roll(second, HALF, 1)

        def spread(value, block):
            if 0 <= block < NB:
                return jnp.broadcast_to(value[:, block : block + 1], (count, LANES))
            return jnp.zeros((count, LANES), jnp.float32)

        for m in range(padded // LANES):
            value = first_turned * jnp.where(left, spread(real, 2 * m - 1), spread(real, 2 * m + 1))
            value += second_turned * jnp.where(
                left, spread(imag, 2 * m - 1), spread(imag, 2 * m + 1)
            )
            if 2 * m < NB:
                value += first * spread(real, 2 * m) + second * spread(imag, 2 * m)
            high, low = split(value)
            own = pl.ds(m * LANES, LANES)
            a_ref[pl.ds(q * count, count), own] = high
            a_ref[pl.ds(total + q * count, count), own] = low
    both = jnp.dot(a_ref[...], high_ref[...], preferred_element_type=jnp.float32)
    modes = both[:total] + both[total:] - jnp.concatenate(corrections, axis=0)
    modes += jnp.dot(a_ref[pl.ds(0, total), :], low_ref[...], preferred_element_type=jnp.float32)
    modes = modes * jnp.sqrt(2.0 * total_rows / load_weights(w_ref, cols // LANES))
    for q in range(PACK):
        for part in range(2):
            rows = q * count + part * groups
            for c in range(cols // LANES):
                out_ref[2 * c + part, pl.ds(q, groups, stride=PACK), :] = modes[
                    rows : rows + groups, c * LANES : (c + 1) * LANES
                ]


def local_modes(high, low, rest, weight_rows, response, total_rows, slot):
    padded, cols = high.shape
    count = NF if slot is None else NF // 2
    return pl.pallas_call(
        functools.partial(modes_kernel, total_rows, slot),
        out_shape=floats(2 * cols // LANES, count, LANES),
        in_specs=[VMEM] * 6,
        out_specs=VMEM,
        scratch_shapes=[pltpu.VMEM((4 * count, padded), jnp.bfloat16)],
        compiler_params=pltpu.CompilerParams(vmem_limit_bytes=MODES_LIMIT),
        cost_estimate=pl.CostEstimate(
            flops=2_000_000_000, bytes_accessed=6_000_000, transcendentals=0
        ),
        name="own_modes" if slot == 0 else "sent_modes",
    )(high, low, rest, weight_rows, jnp.asarray(mode_tables()), response)


def join_kernel(kept_ref, got_ref, out_ref):
    tiles = got_ref.shape[0] // 2
    group = lax.axis_index("freq")
    for slot, ref in enumerate((kept_ref, got_ref)):
        for c in range(tiles):
            lanes = pl.ds(pl.multiple_of(((group ^ slot) * tiles + c) * LANES, LANES), LANES)
            for part in range(2):
                out_ref[:, part, lanes] = ref[2 * c + part]


def join_modes(kept, got):
    tiles, count, _ = got.shape
    return small_call(join_kernel, "join_modes", floats(count, 2, tiles * LANES))(kept, got)


def response_of(gram, start_vec):
    matvec = functools.partial(jnp.einsum, "fjk,fk->fj", precision=lax.Precision.HIGHEST)
    resp_real = matvec(gram[:, 0], start_vec[:, 0]) - matvec(gram[:, 1], start_vec[:, 1])
    resp_imag = matvec(gram[:, 0], start_vec[:, 1]) + matvec(gram[:, 1], start_vec[:, 0])
    scaling = 1.0 / jnp.sqrt(
        jnp.mean(resp_real * resp_real + resp_imag * resp_imag, axis=1, keepdims=True) + 1e-06
    )
    return jnp.stack([resp_real * scaling, resp_imag * scaling], axis=1)


def direction_shards(n_devices, snapshots, weight, start_vec):
    def swap(value, mask):
        return lax.ppermute(value, ("pts", "freq"), [(i, i ^ mask) for i in range(n_devices)])

    x, core, y, z_near, z_far = 1, 2, 4, 8, 16
    near = [
        [first + far, first + far + x, first + far + y, first + far + y + x]
        for far in range(0, n_devices, z_near)
        for first in (0, core)
    ]
    total_rows = float(weight.shape[0] * 16)
    weight_rows = weight.reshape(-1, LANES)
    places = [
        (i // 8 % 2) * 16 + (i // 4 % 2) * 8 + (i // 16) * 4 + i % 4 for i in range(NF // 2)
    ]
    keep, send, high, rest, low = gram_parts(
        snapshots, weight_rows, start_vec, total_rows, places, True
    )
    parts = add_core(keep, swap(send, core))
    parts = lax.all_to_all(
        parts, ("pts", "freq"), 0, 0, axis_index_groups=near, tiled=True
    )
    part = small_call(add_near_kernel, "add_near", floats(*parts.shape[1:]))(parts)
    part = add("add_z", part, swap(part, z_near))
    got = swap(part, z_far)
    low, token = hand_on(low, part)
    got, token = lax.optimization_barrier((got, token))
    packed, response = finish(part, got)
    other = swap(packed, y)
    modes_args = (high, low, rest, weight_rows, response, total_rows)
    got = swap(local_modes(*modes_args, 1), x)
    kept = local_modes(*modes_args, 0)
    other, kept = lax.optimization_barrier((other, kept))
    packed = small_call(join_y_kernel, "join_y", floats(2 * packed.shape[0], LANES))(packed, other)
    gram_mine = unpack_gram(packed, 0)
    gram_mine = unpack_gram(swap(packed, core), 1, gram_mine)
    gram_mine, got = lax.optimization_barrier((gram_mine, got))
    return gram_mine, join_modes(kept, got)


def shards(n_pts, n_freq, snapshots, weight, start_vec):
    cols = snapshots.shape[1]
    total_rows = float(weight.shape[0] * n_pts)
    n_devices = n_pts * n_freq
    mine_count = NF // n_freq
    group = lax.axis_index("freq")
    weight_rows = weight.reshape(-1, LANES)
    places = list(range(NF // 2))
    first, second, high, rest, low = gram_parts(
        snapshots, weight_rows, start_vec, total_rows, places, False
    )
    parts = jnp.concatenate([first[:-RESP_ROWS], second[:-RESP_ROWS]], axis=0)
    share = parts.reshape(n_devices, -1)
    share = jnp.sum(lax.all_to_all(share, ("freq", "pts"), 0, 0, tiled=True), axis=0)
    packed = lax.all_gather(share, "pts", axis=0, tiled=True)
    gram_mine = unpack_gram(packed.reshape(-1, LANES))
    start_mine = lax.dynamic_slice_in_dim(start_vec, group * mine_count, mine_count, 0)
    response = lax.all_gather(response_of(gram_mine, start_mine), "freq", axis=0, tiled=True)
    response = jnp.transpose(response.reshape(NF // PACK, PACK, 2, NB), (2, 0, 1, 3))
    response = response.reshape(RESP_ROWS, LANES)
    modes = local_modes(high, low, rest, weight_rows, response, total_rows, None)
    modes = modes.reshape(-1, n_freq, mine_count, LANES)
    modes = lax.all_to_all(jnp.moveaxis(modes, 1, 0), "freq", 0, 0, tiled=True)
    modes = modes.reshape(n_freq, cols // LANES, 2, mine_count, LANES)
    modes = jnp.transpose(modes, (3, 2, 0, 1, 4)).reshape(mine_count, 2, n_freq * cols)
    return gram_mine, modes


def solution(mesh):
    n_pts, n_freq = mesh.shape["pts"], mesh.shape["freq"]
    if (n_pts, n_freq) == (16, 2):
        body = functools.partial(direction_shards, n_pts * n_freq)
    else:
        body = functools.partial(shards, n_pts, n_freq)
    placed = (P(None, ("pts", "freq")), P("pts"), P())
    return jax.shard_map(
        body,
        mesh=mesh,
        in_specs=placed,
        out_specs=(P("freq", None, None, None), P("freq", None, "pts")),
        check_vma=False,
    )
```

profile of v0, /device:TPU:0, one launch (start us, length us, event | category | flops | bytes accessed | tf_op | source)
XLA Modules:
  0.0 39.4 jit_solution(17556531529398341653)
XLA Ops:
  0.6 0.8 %select_maximum_fusion.aux_ref = f32[70,128]{1,0:T(8,128)S(1)} fusion(f32[64,64]{1,0:T(8,128)} %bitcast.7, f32[6,128]{1,0:T(8,128)} %bitcast.4), kind=kLoop, calls=%fused_computation | loop fusion | flops 26880 | bytes 55296 | tf_op jit(solution)/shard_map/concatenate | solution.py:344
  1.4 9.2 %gram_parts.1 = (f32[288,128]{1,0:T(8,128)S(1)}, f32[288,128]{1,0:T(8,128)S(1)}, bf16[2176,384]{1,0:T(8,128)(2,1)S(1)}, f32[8,384]{1,0:T(8,128)S(1)}, bf16[2176,384]{1,0:T(8,128)(2,1)}) custom-call(f32[2112,384]{1,0:T(8,128)} %x_hbm.1, f32[70,128]{1,0:T(8,128)S(1)} %select_maximum_fusion.aux_ref), custom_call_target="tpu_custom_call" | custom-call | flops 5000000000 | bytes 8000000 | tf_op jit(solution)/shard_map/gram_parts/pallas_call | solution.py:348
  10.7 0.0 copy-start.1
  10.7 0.0 copy-start.2
  10.7 0.5 %collective-permute-start = (f32[288,128]{1,0:T(8,128)S(1)}, f32[288,128]{1,0:T(8,128)S(1)}, u32[]{:S(2)}, u32[]{:S(2)}) collective-permute-start(f32[288,128]{1,0:T(8,128)S(1)} %get-tuple-element.15), channel_id=1, source_target_pairs={{0,2},{1,3},{2,0},{3,1},{4,6},{5,7},{6,4},{7,5},{8,10},{9,11},{10,... | collective-permute-start | bytes 442376 | tf_op jit(solution)/shard_map/ppermute | solution.py:652
  11.2 1.0 %collective-permute-done.got_ref = f32[288,128]{1,0:T(8,128)S(1)} collective-permute-done((f32[288,128]{1,0:T(8,128)S(1)}, f32[288,128]{1,0:T(8,128)S(1)}, u32[]{:S(2)}, u32[]{:S(2)}) %collective-permute-start) | collective-permute-done | bytes 147488 | tf_op jit(solution)/shard_map/ppermute | solution.py:652
  12.2 10.4 %all_to_all.5.parts_ref = f32[4,96,128]{2,1,0:T(8,128)S(1)} all-to-all(f32[4,96,128]{2,1,0:T(8,128)S(1)} %add_core.1), channel_id=1, replica_groups={{0,1,4,5},{2,3,6,7},{8,9,12,13},{10,11,14,15},{16,17,20,21},{18,19,22,2..., dimensions={0} | all-to-all | bytes 393216 | tf_op jit(solution)/shard_map/all_to_all | solution.py:669
  22.7 1.6 %collective-permute-start.1 = (f32[96,128]{1,0:T(8,128)S(1)}, f32[96,128]{1,0:T(8,128)S(1)}, u32[]{:S(2)}, u32[]{:S(2)}) collective-permute-start(f32[96,128]{1,0:T(8,128)S(1)} %add_near.1.kept_ref), channel_id=1, source_target_pairs={{0,8},{1,9},{2,10},{3,11},{4,12},{5,13},{6,14},{7,15},{8,0},{9,1},... | collective-permute-start | bytes 147464 | tf_op jit(solution)/shard_map/ppermute | solution.py:652
  24.3 2.5 %collective-permute-done.1.got_ref = f32[96,128]{1,0:T(8,128)S(1)} collective-permute-done((f32[96,128]{1,0:T(8,128)S(1)}, f32[96,128]{1,0:T(8,128)S(1)}, u32[]{:S(2)}, u32[]{:S(2)}) %collective-permute-start.1) | collective-permute-done | bytes 49184 | tf_op jit(solution)/shard_map/ppermute | solution.py:652
  26.8 2.6 %collective-permute-start.2 = (f32[96,128]{1,0:T(8,128)S(1)}, f32[96,128]{1,0:T(8,128)S(1)}, u32[]{:S(2)}, u32[]{:S(2)}) collective-permute-start(f32[96,128]{1,0:T(8,128)S(1)} %add_z.1.kept_ref.after_ref), channel_id=1, source_target_pairs={{0,16},{1,17},{2,18},{3,19},{4,20},{5,21},{6,22},{7,23},{8,24},{9,... | collective-permute-start | bytes 147464 | tf_op jit(solution)/shard_map/ppermute | solution.py:652
  29.5 0.0 copy-start
  29.5 1.4 %copy-done = bf16[2176,384]{1,0:T(8,128)(2,1)S(1)} copy-done((bf16[2176,384]{1,0:T(8,128)(2,1)S(1)}, bf16[2176,384]{1,0:T(8,128)(2,1)}, u32[]{:S(2)}) %copy-start) | copy-done | bytes 1671192
  30.9 0.8 %hand_on.1 = (bf16[2176,384]{1,0:T(8,128)(2,1)S(1)}, f32[8,128]{1,0:T(8,128)}) custom-call(bf16[2176,384]{1,0:T(8,128)(2,1)S(1)} %copy-done, f32[96,128]{1,0:T(8,128)S(1)} %add_z.1.kept_ref.after_ref), custom_call_target="tpu_custom_call" | custom-call | tf_op jit(solution)/shard_map/hand_on/pallas_call | solution.py:521
  31.8 0.1 collective-permute-done.2.got_ref
  31.9 0.1 finish.1
  32.0 0.8 %collective-permute-start.3 = (f32[64,128]{1,0:T(8,128)S(1)}, f32[64,128]{1,0:T(8,128)S(1)}, u32[]{:S(2)}, u32[]{:S(2)}) collective-permute-start(f32[64,128]{1,0:T(8,128)S(1)} %get-tuple-element.16.own_ref), channel_id=1, source_target_pairs={{0,4},{1,5},{2,6},{3,7},{4,0},{5,1},{6,2},{7,3},{8,12},{9,13},{10,... | collective-permute-start | bytes 98312 | tf_op jit(solution)/shard_map/ppermute | solution.py:652
  32.8 0.0 copy-done.1
  32.8 0.0 copy-done.2
  32.8 1.1 %sent_modes.1 = f32[6,32,128]{2,1,0:T(8,128)S(1)} custom-call(bf16[2176,384]{1,0:T(8,128)(2,1)S(1)} %get-tuple-element.17.high_ref, bf16[2176,384]{1,0:T(8,128)(2,1)S(1)} %get-tuple-element.19.low_ref, f32[8,384]{1,0:T(8,128)S(1)} %get-tuple-element.20.rest_ref, f32[6,128]{1,0:T(8,128)S(1)} %bitcast.5, f32[2,128,128]{2,1,0:T(8,128)S(1)} %copy-done.2, ...), custom_call_target="tpu_custom_call" | custom-call | flops 2000000000 | bytes 6000000 | tf_op jit(solution)/shard_map/sent_modes/pallas_call | solution.py:611
  33.9 0.6 %collective-permute-start.5 = (f32[6,32,128]{2,1,0:T(8,128)S(1)}, f32[6,32,128]{2,1,0:T(8,128)S(1)}, u32[]{:S(2)}, u32[]{:S(2)}) collective-permute-start(f32[6,32,128]{2,1,0:T(8,128)S(1)} %sent_modes.1), channel_id=1, source_target_pairs={{0,1},{1,0},{2,3},{3,2},{4,5},{5,4},{6,7},{7,6},{8,9},{9,8},{10,11... | collective-permute-start | bytes 294920 | tf_op jit(solution)/shard_map/ppermute | solution.py:652
  34.5 1.1 %own_modes.1.kept_ref = f32[6,32,128]{2,1,0:T(8,128)S(1)} custom-call(bf16[2176,384]{1,0:T(8,128)(2,1)S(1)} %get-tuple-element.17.high_ref, bf16[2176,384]{1,0:T(8,128)(2,1)S(1)} %get-tuple-element.19.low_ref, f32[8,384]{1,0:T(8,128)S(1)} %get-tuple-element.20.rest_ref, f32[6,128]{1,0:T(8,128)S(1)} %bitcast.6, f32[2,128,128]{2,1,0:T(8,128)S(1)} %copy-done.2, ...), custom_call_target="tpu_custom_call" | custom-call | flops 2000000000 | bytes 6000000 | tf_op jit(solution)/shard_map/own_modes/pallas_call | solution.py:611
  35.6 0.3 collective-permute-done.3.got_ref
  36.0 0.1 collective-permute-start.4
  36.1 1.2 %unpack_own.1.refs_0_ = f32[32,2,32,32]{3,2,1,0:T(8,128)} custom-call(f32[128,128]{1,0:T(8,128)S(1)} %join_y.1.refs_0_), custom_call_target="tpu_custom_call" | custom-call | tf_op jit(solution)/shard_map/unpack_own/pallas_call | solution.py:498
  37.3 0.0 collective-permute-done.4.refs_1_
  37.3 1.2 %unpack_other.1 = f32[32,2,32,32]{3,2,1,0:T(8,128)} custom-call(f32[32,2,32,32]{3,2,1,0:T(8,128)} %unpack_own.1.refs_0_, f32[128,128]{1,0:T(8,128)S(1)} %collective-permute-done.4.refs_1_), custom_call_target="tpu_custom_call", output_to_operand_aliasing={{}: (0, {})} | custom-call | tf_op jit(solution)/shard_map/unpack_other/pallas_call | solution.py:498
  38.5 0.1 collective-permute-done.5.got_ref
  38.6 0.8 %join_modes.1 = f32[32,2,768]{2,1,0:T(2,128)} custom-call(f32[6,32,128]{2,1,0:T(8,128)S(1)} %own_modes.1.kept_ref, f32[6,32,128]{2,1,0:T(8,128)S(1)} %collective-permute-done.5.got_ref), custom_call_target="tpu_custom_call" | custom-call | tf_op jit(solution)/shard_map/join_modes/pallas_call | solution.py:398
  (4 shorter events, 0.0 us)
Async XLA Ops:
  10.7 22.1 %copy-start.1 = (f32[768]{0:T(1024)S(1)}, f32[768]{0:T(1024)}, u32[]{:S(2)}) copy-start(f32[768]{0:T(1024)} %param.6) | copy-start | bytes 9220
  10.7 22.1 %copy-start.2 = (f32[2,128,128]{2,1,0:T(8,128)S(1)}, f32[2,128,128]{2,1,0:T(8,128)}, u32[]{:S(2)}) copy-start(f32[2,128,128]{2,1,0:T(8,128)} %constant.5.clone.table_ref) | copy-start | bytes 393220
  10.7 1.5 %collective-permute-start = (f32[288,128]{1,0:T(8,128)S(1)}, f32[288,128]{1,0:T(8,128)S(1)}, u32[]{:S(2)}, u32[]{:S(2)}) collective-permute-start(f32[288,128]{1,0:T(8,128)S(1)} %get-tuple-element.15), channel_id=1, source_target_pairs={{0,2},{1,3},{2,0},{3,1},{4,6},{5,7},{6,4},{7,5},{8,10},{9,11},{10,... | collective-permute-start | bytes 442376 | tf_op jit(solution)/shard_map/ppermute | solution.py:652
  22.7 4.2 %collective-permute-start.1 = (f32[96,128]{1,0:T(8,128)S(1)}, f32[96,128]{1,0:T(8,128)S(1)}, u32[]{:S(2)}, u32[]{:S(2)}) collective-permute-start(f32[96,128]{1,0:T(8,128)S(1)} %add_near.1.kept_ref), channel_id=1, source_target_pairs={{0,8},{1,9},{2,10},{3,11},{4,12},{5,13},{6,14},{7,15},{8,0},{9,1},... | collective-permute-start | bytes 147464 | tf_op jit(solution)/shard_map/ppermute | solution.py:652
  26.8 5.0 %collective-permute-start.2 = (f32[96,128]{1,0:T(8,128)S(1)}, f32[96,128]{1,0:T(8,128)S(1)}, u32[]{:S(2)}, u32[]{:S(2)}) collective-permute-start(f32[96,128]{1,0:T(8,128)S(1)} %add_z.1.kept_ref.after_ref), channel_id=1, source_target_pairs={{0,16},{1,17},{2,18},{3,19},{4,20},{5,21},{6,22},{7,23},{8,24},{9,... | collective-permute-start | bytes 147464 | tf_op jit(solution)/shard_map/ppermute | solution.py:652
  29.5 1.4 %copy-start = (bf16[2176,384]{1,0:T(8,128)(2,1)S(1)}, bf16[2176,384]{1,0:T(8,128)(2,1)}, u32[]{:S(2)}) copy-start(bf16[2176,384]{1,0:T(8,128)(2,1)} %get-tuple-element.18.low_hbm) | copy-start | bytes 5013508
  32.0 4.0 %collective-permute-start.3 = (f32[64,128]{1,0:T(8,128)S(1)}, f32[64,128]{1,0:T(8,128)S(1)}, u32[]{:S(2)}, u32[]{:S(2)}) collective-permute-start(f32[64,128]{1,0:T(8,128)S(1)} %get-tuple-element.16.own_ref), channel_id=1, source_target_pairs={{0,4},{1,5},{2,6},{3,7},{4,0},{5,1},{6,2},{7,3},{8,12},{9,13},{10,... | collective-permute-start | bytes 98312 | tf_op jit(solution)/shard_map/ppermute | solution.py:652
  33.9 4.7 %collective-permute-start.5 = (f32[6,32,128]{2,1,0:T(8,128)S(1)}, f32[6,32,128]{2,1,0:T(8,128)S(1)}, u32[]{:S(2)}, u32[]{:S(2)}) collective-permute-start(f32[6,32,128]{2,1,0:T(8,128)S(1)} %sent_modes.1), channel_id=1, source_target_pairs={{0,1},{1,0},{2,3},{3,2},{4,5},{5,4},{6,7},{7,6},{8,9},{9,8},{10,11... | collective-permute-start | bytes 294920 | tf_op jit(solution)/shard_map/ppermute | solution.py:652
  36.0 1.3 %collective-permute-start.4 = (f32[128,128]{1,0:T(8,128)S(1)}, f32[128,128]{1,0:T(8,128)S(1)}, u32[]{:S(2)}, u32[]{:S(2)}) collective-permute-start(f32[128,128]{1,0:T(8,128)S(1)} %join_y.1.refs_0_), channel_id=1, source_target_pairs={{0,2},{1,3},{2,0},{3,1},{4,6},{5,7},{6,4},{7,5},{8,10},{9,11},{10,... | collective-permute-start | bytes 196616 | tf_op jit(solution)/shard_map/ppermute | solution.py:652
where the time goes:
time: 39.7 us; the launch traced here: 39.4 us
  Pallas kernels  15.7 us (40%)
  blocking collectives  10.4 us (26%)
  starting transfers between devices  6.31 us (16%)
  waiting for transfers between devices  4.03 us (10%)
  local copies, waits for them, and re-layouts  1.45 us (4%)
  other arithmetic  0.77 us (2%)
  between operations  0.73 us (2%)
    all_to_all x1, blocking collectives, direction_shards(): lax.all_to_all(parts, ('pts', 'freq'), 0, 0, axis_index_groups=near, tile...  10.4 us
    pallas_call x1, Pallas kernels, gram_parts(): pl.pallas_call(functools.partial(gram_kernel, total_rows, places, by_core...  9.25 us
    ppermute x6, starting transfers between devices, swap(): lax.ppermute(value, ('pts', 'freq'), [(i, i ^ mask) for i in range(n_devi...  6.31 us
    ppermute x6, waiting for transfers between devices, swap(): lax.ppermute(value, ('pts', 'freq'), [(i, i ^ mask) for i in range(n_devi...  4.03 us
    pallas_call x2, Pallas kernels, unpack_gram(): pl.pallas_call(functools.partial(unpack_kernel, part_index), out_shape=fl...  2.45 us
    pallas_call x2, Pallas kernels, local_modes(): pl.pallas_call(functools.partial(modes_kernel, total_rows, slot), out_sha...  2.21 us
    unnamed x6, local copies, waits for them, and re-layouts  1.45 us
    pallas_call x6, Pallas kernels, call(): pl.pallas_call(kernel, out_shape=out_shape, in_specs=[VMEM] * len(args),...  0.95 us
  transfers between devices with their start and end apart: 6, of which 5 were waited for; matrix products, arithmetic and copies ran while one was open for 0% of the time, Pallas kernels for 14%

commit v1 on v0

--- a/solution.py
+++ b/solution.py
@@ -412,23 +412,17 @@
     return jax.ShapeDtypeStruct(shape, jnp.float32)
 
 
-def add_core_kernel(kept_ref, got_ref, out_ref):
-    quarter = out_ref.shape[1] - RESP_ROWS
-    tail = pl.ds(4 * quarter, RESP_ROWS)
-    resp = kept_ref[tail, :] + got_ref[tail, :]
-    for m in range(4):
-        rows = pl.ds(m * quarter, quarter)
-        out_ref[m, pl.ds(0, quarter), :] = kept_ref[rows, :] + got_ref[rows, :]
-        out_ref[m, pl.ds(quarter, RESP_ROWS), :] = resp
-
-
-def add_core(kept, got):
-    quarter = (kept.shape[0] - RESP_ROWS) // 4
-    return small_call(add_core_kernel, "add_core", floats(4, quarter + RESP_ROWS, LANES))(kept, got)
-
-
-def add_near_kernel(parts_ref, out_ref):
-    out_ref[...] = (parts_ref[0] + parts_ref[1]) + (parts_ref[2] + parts_ref[3])
+def add_split_kernel(bit, kept_ref, got_ref, keep_ref, send_ref, sum_ref):
+    sum_ref[...] = kept_ref[...] + got_ref[...]
+    give_half(sum_ref, bit(), keep_ref, send_ref)
+
+
+def add_split(bit, name, kept, got):
+    half = floats((kept.shape[0] - RESP_ROWS) // 2 + RESP_ROWS, LANES)
+    scratch = [pltpu.VMEM(kept.shape, jnp.float32)]
+    return small_call(functools.partial(add_split_kernel, bit), name, (half, half), scratch)(
+        kept, got
+    )
 
 
 def add_kernel(kept_ref, got_ref, out_ref):
@@ -652,24 +646,15 @@
         return lax.ppermute(value, ("pts", "freq"), [(i, i ^ mask) for i in range(n_devices)])
 
     x, core, y, z_near, z_far = 1, 2, 4, 8, 16
-    near = [
-        [first + far, first + far + x, first + far + y, first + far + y + x]
-        for far in range(0, n_devices, z_near)
-        for first in (0, core)
-    ]
     total_rows = float(weight.shape[0] * 16)
     weight_rows = weight.reshape(-1, LANES)
-    places = [
-        (i // 8 % 2) * 16 + (i // 4 % 2) * 8 + (i // 16) * 4 + i % 4 for i in range(NF // 2)
-    ]
+    places = [(i // 8 % 2) * 16 + (i // 16) * 8 + i % 8 for i in range(NF // 2)]
     keep, send, high, rest, low = gram_parts(
         snapshots, weight_rows, start_vec, total_rows, places, True
     )
-    parts = add_core(keep, swap(send, core))
-    parts = lax.all_to_all(
-        parts, ("pts", "freq"), 0, 0, axis_index_groups=near, tiled=True
-    )
-    part = small_call(add_near_kernel, "add_near", floats(*parts.shape[1:]))(parts)
+    keep, send = add_split(lambda: lax.axis_index("freq"), "add_core", keep, swap(send, core))
+    keep, send = add_split(y_bit, "add_x", keep, swap(send, x))
+    part = add("add_y", keep, swap(send, y))
     part = add("add_z", part, swap(part, z_near))
     got = swap(part, z_far)
     low, token = hand_on(low, part)

time: 39.7 us -> 41 us (1.033)
  blocking collectives: 10.4 us -> 0 us
  starting transfers between devices: 6.31 us -> 13.7 us
  waiting for transfers between devices: 4.03 us -> 8.36 us
    all_to_all x1 -> x0, blocking collectives: 10.4 us -> none  [direction_shards(): lax.all_to_all(parts, ('pts', 'freq'), 0, 0, axis_index_groups=near, tile...]
    ppermute x6 -> x8, starting transfers between devices: 6.31 us -> 13.7 us  [swap(): lax.ppermute(value, ('pts', 'freq'), [(i, i ^ mask) for i in range(n_devi...]
    ppermute x6 -> x8, waiting for transfers between devices: 4.03 us -> 8.36 us  [swap(): lax.ppermute(value, ('pts', 'freq'), [(i, i ^ mask) for i in range(n_devi...]
    pallas_call x6 -> x7, Pallas kernels: 0.95 us -> 0.99 us  [call(): pl.pallas_call(kernel, out_shape=out_shape, in_specs=[VMEM] * len(args),...]
  transfers between devices with their start and end apart: 6 -> 8, of which waited for: 5 -> 4; matrix products, arithmetic and copies ran while one was open for 0% -> 0% of each run, Pallas kernels for 14% -> 14%
where the time goes in v1:
time: 41 us; the launch traced here: 40.8 us
  Pallas kernels  15.7 us (38%)
  starting transfers between devices  13.7 us (33%)
  waiting for transfers between devices  8.36 us (20%)
  local copies, waits for them, and re-layouts  1.45 us (4%)
  other arithmetic  0.77 us (2%)
  between operations  0.76 us (2%)
    ppermute x8, starting transfers between devices, swap(): lax.ppermute(value, ('pts', 'freq'), [(i, i ^ mask) for i in range(n_devi...  13.7 us
    pallas_call x1, Pallas kernels, gram_parts(): pl.pallas_call(functools.partial(gram_kernel, total_rows, places, by_core...  9.24 us
    ppermute x8, waiting for transfers between devices, swap(): lax.ppermute(value, ('pts', 'freq'), [(i, i ^ mask) for i in range(n_devi...  8.36 us
    pallas_call x2, Pallas kernels, unpack_gram(): pl.pallas_call(functools.partial(unpack_kernel, part_index), out_shape=fl...  2.45 us
    pallas_call x2, Pallas kernels, local_modes(): pl.pallas_call(functools.partial(modes_kernel, total_rows, slot), out_sha...  2.21 us
    unnamed x6, local copies, waits for them, and re-layouts  1.45 us
    pallas_call x7, Pallas kernels, call(): pl.pallas_call(kernel, out_shape=out_shape, in_specs=[VMEM] * len(args),...  0.99 us
    pallas_call x1, Pallas kernels, hand_on(): pl.pallas_call(hand_on_kernel, out_shape=(jax.ShapeDtypeStruct(low.shape,...  0.83 us
  transfers between devices with their start and end apart: 8, of which 4 were waited for; matrix products, arithmetic and copies ran while one was open for 0% of the time, Pallas kernels for 14%

profile of v1, /device:TPU:0, one launch (start us, length us, event | category | flops | bytes accessed | tf_op | source)
XLA Modules:
  0.0 40.8 jit_solution(13707360368691876334)
XLA Ops:
  0.6 0.8 %select_maximum_fusion.aux_ref = f32[70,128]{1,0:T(8,128)S(1)} fusion(f32[64,64]{1,0:T(8,128)} %bitcast.7, f32[6,128]{1,0:T(8,128)} %bitcast.4), kind=kLoop, calls=%fused_computation | loop fusion | flops 26880 | bytes 55296 | tf_op jit(solution)/shard_map/concatenate | solution.py:344
  1.4 9.2 %gram_parts.1 = (f32[288,128]{1,0:T(8,128)S(1)}, f32[288,128]{1,0:T(8,128)S(1)}, bf16[2176,384]{1,0:T(8,128)(2,1)S(1)}, f32[8,384]{1,0:T(8,128)S(1)}, bf16[2176,384]{1,0:T(8,128)(2,1)}) custom-call(f32[2112,384]{1,0:T(8,128)} %x_hbm.1, f32[70,128]{1,0:T(8,128)S(1)} %select_maximum_fusion.aux_ref), custom_call_target="tpu_custom_call" | custom-call | flops 5000000000 | bytes 8000000 | tf_op jit(solution)/shard_map/gram_parts/pallas_call | solution.py:348
  10.6 0.0 copy-start.1
  10.7 0.0 copy-start.2
  10.7 0.5 %collective-permute-start = (f32[288,128]{1,0:T(8,128)S(1)}, f32[288,128]{1,0:T(8,128)S(1)}, u32[]{:S(2)}, u32[]{:S(2)}) collective-permute-start(f32[288,128]{1,0:T(8,128)S(1)} %get-tuple-element.19), channel_id=1, source_target_pairs={{0,2},{1,3},{2,0},{3,1},{4,6},{5,7},{6,4},{7,5},{8,10},{9,11},{10,... | collective-permute-start | bytes 442376 | tf_op jit(solution)/shard_map/ppermute | solution.py:646
  11.2 1.0 %collective-permute-done.got_ref = f32[288,128]{1,0:T(8,128)S(1)} collective-permute-done((f32[288,128]{1,0:T(8,128)S(1)}, f32[288,128]{1,0:T(8,128)S(1)}, u32[]{:S(2)}, u32[]{:S(2)}) %collective-permute-start) | collective-permute-done | bytes 147488 | tf_op jit(solution)/shard_map/ppermute | solution.py:646
  12.2 2.9 %collective-permute-start.1 = (f32[160,128]{1,0:T(8,128)S(1)}, f32[160,128]{1,0:T(8,128)S(1)}, u32[]{:S(2)}, u32[]{:S(2)}) collective-permute-start(f32[160,128]{1,0:T(8,128)S(1)} %get-tuple-element.21), channel_id=1, source_target_pairs={{0,1},{1,0},{2,3},{3,2},{4,5},{5,4},{6,7},{7,6},{8,9},{9,8},{10,11... | collective-permute-start | bytes 245768 | tf_op jit(solution)/shard_map/ppermute | solution.py:646
  15.1 2.8 %collective-permute-done.1.got_ref = f32[160,128]{1,0:T(8,128)S(1)} collective-permute-done((f32[160,128]{1,0:T(8,128)S(1)}, f32[160,128]{1,0:T(8,128)S(1)}, u32[]{:S(2)}, u32[]{:S(2)}) %collective-permute-start.1) | collective-permute-done | bytes 81952 | tf_op jit(solution)/shard_map/ppermute | solution.py:646
  17.9 1.8 %collective-permute-start.2 = (f32[96,128]{1,0:T(8,128)S(1)}, f32[96,128]{1,0:T(8,128)S(1)}, u32[]{:S(2)}, u32[]{:S(2)}) collective-permute-start(f32[96,128]{1,0:T(8,128)S(1)} %get-tuple-element.23), channel_id=1, source_target_pairs={{0,4},{1,5},{2,6},{3,7},{4,0},{5,1},{6,2},{7,3},{8,12},{9,13},{10,... | collective-permute-start | bytes 147464 | tf_op jit(solution)/shard_map/ppermute | solution.py:646
  19.8 2.3 %collective-permute-done.2.got_ref = f32[96,128]{1,0:T(8,128)S(1)} collective-permute-done((f32[96,128]{1,0:T(8,128)S(1)}, f32[96,128]{1,0:T(8,128)S(1)}, u32[]{:S(2)}, u32[]{:S(2)}) %collective-permute-start.2) | collective-permute-done | bytes 49184 | tf_op jit(solution)/shard_map/ppermute | solution.py:646
  22.1 1.9 %collective-permute-start.3 = (f32[96,128]{1,0:T(8,128)S(1)}, f32[96,128]{1,0:T(8,128)S(1)}, u32[]{:S(2)}, u32[]{:S(2)}) collective-permute-start(f32[96,128]{1,0:T(8,128)S(1)} %add_y.1.kept_ref), channel_id=1, source_target_pairs={{0,8},{1,9},{2,10},{3,11},{4,12},{5,13},{6,14},{7,15},{8,0},{9,1},... | collective-permute-start | bytes 147464 | tf_op jit(solution)/shard_map/ppermute | solution.py:646
  24.0 2.3 %collective-permute-done.3.got_ref = f32[96,128]{1,0:T(8,128)S(1)} collective-permute-done((f32[96,128]{1,0:T(8,128)S(1)}, f32[96,128]{1,0:T(8,128)S(1)}, u32[]{:S(2)}, u32[]{:S(2)}) %collective-permute-start.3) | collective-permute-done | bytes 49184 | tf_op jit(solution)/shard_map/ppermute | solution.py:646
  26.2 3.3 %collective-permute-start.4 = (f32[96,128]{1,0:T(8,128)S(1)}, f32[96,128]{1,0:T(8,128)S(1)}, u32[]{:S(2)}, u32[]{:S(2)}) collective-permute-start(f32[96,128]{1,0:T(8,128)S(1)} %add_z.1.kept_ref.after_ref), channel_id=1, source_target_pairs={{0,16},{1,17},{2,18},{3,19},{4,20},{5,21},{6,22},{7,23},{8,24},{9,... | collective-permute-start | bytes 147464 | tf_op jit(solution)/shard_map/ppermute | solution.py:646
  29.6 0.0 copy-start
  29.6 1.4 %copy-done = bf16[2176,384]{1,0:T(8,128)(2,1)S(1)} copy-done((bf16[2176,384]{1,0:T(8,128)(2,1)S(1)}, bf16[2176,384]{1,0:T(8,128)(2,1)}, u32[]{:S(2)}) %copy-start) | copy-done | bytes 1671192
  31.0 0.8 %hand_on.1 = (bf16[2176,384]{1,0:T(8,128)(2,1)S(1)}, f32[8,128]{1,0:T(8,128)}) custom-call(bf16[2176,384]{1,0:T(8,128)(2,1)S(1)} %copy-done, f32[96,128]{1,0:T(8,128)S(1)} %add_z.1.kept_ref.after_ref), custom_call_target="tpu_custom_call" | custom-call | tf_op jit(solution)/shard_map/hand_on/pallas_call | solution.py:515
  31.9 0.0 collective-permute-done.4.got_ref
  31.9 0.1 finish.1
  32.0 1.6 %collective-permute-start.5 = (f32[64,128]{1,0:T(8,128)S(1)}, f32[64,128]{1,0:T(8,128)S(1)}, u32[]{:S(2)}, u32[]{:S(2)}) collective-permute-start(f32[64,128]{1,0:T(8,128)S(1)} %get-tuple-element.24.own_ref), channel_id=1, source_target_pairs={{0,4},{1,5},{2,6},{3,7},{4,0},{5,1},{6,2},{7,3},{8,12},{9,13},{10,... | collective-permute-start | bytes 98312 | tf_op jit(solution)/shard_map/ppermute | solution.py:646
  33.6 0.0 copy-done.1
  33.6 0.0 copy-done.2
  33.6 1.1 %sent_modes.1 = f32[6,32,128]{2,1,0:T(8,128)S(1)} custom-call(bf16[2176,384]{1,0:T(8,128)(2,1)S(1)} %get-tuple-element.25.high_ref, bf16[2176,384]{1,0:T(8,128)(2,1)S(1)} %get-tuple-element.27.low_ref, f32[8,384]{1,0:T(8,128)S(1)} %get-tuple-element.28.rest_ref, f32[6,128]{1,0:T(8,128)S(1)} %bitcast.5, f32[2,128,128]{2,1,0:T(8,128)S(1)} %copy-done.2, ...), custom_call_target="tpu_custom_call" | custom-call | flops 2000000000 | bytes 6000000 | tf_op jit(solution)/shard_map/sent_modes/pallas_call | solution.py:605
  34.7 1.6 %collective-permute-start.7 = (f32[6,32,128]{2,1,0:T(8,128)S(1)}, f32[6,32,128]{2,1,0:T(8,128)S(1)}, u32[]{:S(2)}, u32[]{:S(2)}) collective-permute-start(f32[6,32,128]{2,1,0:T(8,128)S(1)} %sent_modes.1), channel_id=1, source_target_pairs={{0,1},{1,0},{2,3},{3,2},{4,5},{5,4},{6,7},{7,6},{8,9},{9,8},{10,11... | collective-permute-start | bytes 294920 | tf_op jit(solution)/shard_map/ppermute | solution.py:646
  36.2 1.1 %own_modes.1.kept_ref = f32[6,32,128]{2,1,0:T(8,128)S(1)} custom-call(bf16[2176,384]{1,0:T(8,128)(2,1)S(1)} %get-tuple-element.25.high_ref, bf16[2176,384]{1,0:T(8,128)(2,1)S(1)} %get-tuple-element.27.low_ref, f32[8,384]{1,0:T(8,128)S(1)} %get-tuple-element.28.rest_ref, f32[6,128]{1,0:T(8,128)S(1)} %bitcast.6, f32[2,128,128]{2,1,0:T(8,128)S(1)} %copy-done.2, ...), custom_call_target="tpu_custom_call" | custom-call | flops 2000000000 | bytes 6000000 | tf_op jit(solution)/shard_map/own_modes/pallas_call | solution.py:605
  37.3 0.0 collective-permute-done.5.got_ref
  37.4 0.1 collective-permute-start.6
  37.5 1.2 %unpack_own.1.refs_0_ = f32[32,2,32,32]{3,2,1,0:T(8,128)} custom-call(f32[128,128]{1,0:T(8,128)S(1)} %join_y.1.refs_0_), custom_call_target="tpu_custom_call" | custom-call | tf_op jit(solution)/shard_map/unpack_own/pallas_call | solution.py:492
  38.7 0.0 collective-permute-done.6.refs_1_
  38.7 1.2 %unpack_other.1 = f32[32,2,32,32]{3,2,1,0:T(8,128)} custom-call(f32[32,2,32,32]{3,2,1,0:T(8,128)} %unpack_own.1.refs_0_, f32[128,128]{1,0:T(8,128)S(1)} %collective-permute-done.6.refs_1_), custom_call_target="tpu_custom_call", output_to_operand_aliasing={{}: (0, {})} | custom-call | tf_op jit(solution)/shard_map/unpack_other/pallas_call | solution.py:492
  39.9 0.0 collective-permute-done.7.got_ref
  40.0 0.8 %join_modes.1 = f32[32,2,768]{2,1,0:T(2,128)} custom-call(f32[6,32,128]{2,1,0:T(8,128)S(1)} %own_modes.1.kept_ref, f32[6,32,128]{2,1,0:T(8,128)S(1)} %collective-permute-done.7.got_ref), custom_call_target="tpu_custom_call" | custom-call | tf_op jit(solution)/shard_map/join_modes/pallas_call | solution.py:398
  (5 shorter events, 0.1 us)
Async XLA Ops:
  10.6 22.9 %copy-start.1 = (f32[768]{0:T(1024)S(1)}, f32[768]{0:T(1024)}, u32[]{:S(2)}) copy-start(f32[768]{0:T(1024)} %param.6) | copy-start | bytes 9220
  10.7 22.9 %copy-start.2 = (f32[2,128,128]{2,1,0:T(8,128)S(1)}, f32[2,128,128]{2,1,0:T(8,128)}, u32[]{:S(2)}) copy-start(f32[2,128,128]{2,1,0:T(8,128)} %constant.5.clone.table_ref) | copy-start | bytes 393220
  10.7 1.5 %collective-permute-start = (f32[288,128]{1,0:T(8,128)S(1)}, f32[288,128]{1,0:T(8,128)S(1)}, u32[]{:S(2)}, u32[]{:S(2)}) collective-permute-start(f32[288,128]{1,0:T(8,128)S(1)} %get-tuple-element.19), channel_id=1, source_target_pairs={{0,2},{1,3},{2,0},{3,1},{4,6},{5,7},{6,4},{7,5},{8,10},{9,11},{10,... | collective-permute-start | bytes 442376 | tf_op jit(solution)/shard_map/ppermute | solution.py:646
  12.2 5.7 %collective-permute-start.1 = (f32[160,128]{1,0:T(8,128)S(1)}, f32[160,128]{1,0:T(8,128)S(1)}, u32[]{:S(2)}, u32[]{:S(2)}) collective-permute-start(f32[160,128]{1,0:T(8,128)S(1)} %get-tuple-element.21), channel_id=1, source_target_pairs={{0,1},{1,0},{2,3},{3,2},{4,5},{5,4},{6,7},{7,6},{8,9},{9,8},{10,11... | collective-permute-start | bytes 245768 | tf_op jit(solution)/shard_map/ppermute | solution.py:646
  17.9 4.2 %collective-permute-start.2 = (f32[96,128]{1,0:T(8,128)S(1)}, f32[96,128]{1,0:T(8,128)S(1)}, u32[]{:S(2)}, u32[]{:S(2)}) collective-permute-start(f32[96,128]{1,0:T(8,128)S(1)} %get-tuple-element.23), channel_id=1, source_target_pairs={{0,4},{1,5},{2,6},{3,7},{4,0},{5,1},{6,2},{7,3},{8,12},{9,13},{10,... | collective-permute-start | bytes 147464 | tf_op jit(solution)/shard_map/ppermute | solution.py:646
  22.1 4.2 %collective-permute-start.3 = (f32[96,128]{1,0:T(8,128)S(1)}, f32[96,128]{1,0:T(8,128)S(1)}, u32[]{:S(2)}, u32[]{:S(2)}) collective-permute-start(f32[96,128]{1,0:T(8,128)S(1)} %add_y.1.kept_ref), channel_id=1, source_target_pairs={{0,8},{1,9},{2,10},{3,11},{4,12},{5,13},{6,14},{7,15},{8,0},{9,1},... | collective-permute-start | bytes 147464 | tf_op jit(solution)/shard_map/ppermute | solution.py:646
  26.2 5.6 %collective-permute-start.4 = (f32[96,128]{1,0:T(8,128)S(1)}, f32[96,128]{1,0:T(8,128)S(1)}, u32[]{:S(2)}, u32[]{:S(2)}) collective-permute-start(f32[96,128]{1,0:T(8,128)S(1)} %add_z.1.kept_ref.after_ref), channel_id=1, source_target_pairs={{0,16},{1,17},{2,18},{3,19},{4,20},{5,21},{6,22},{7,23},{8,24},{9,... | collective-permute-start | bytes 147464 | tf_op jit(solution)/shard_map/ppermute | solution.py:646
  29.6 1.4 %copy-start = (bf16[2176,384]{1,0:T(8,128)(2,1)S(1)}, bf16[2176,384]{1,0:T(8,128)(2,1)}, u32[]{:S(2)}) copy-start(bf16[2176,384]{1,0:T(8,128)(2,1)} %get-tuple-element.26.low_hbm) | copy-start | bytes 5013508
  32.0 5.4 %collective-permute-start.5 = (f32[64,128]{1,0:T(8,128)S(1)}, f32[64,128]{1,0:T(8,128)S(1)}, u32[]{:S(2)}, u32[]{:S(2)}) collective-permute-start(f32[64,128]{1,0:T(8,128)S(1)} %get-tuple-element.24.own_ref), channel_id=1, source_target_pairs={{0,4},{1,5},{2,6},{3,7},{4,0},{5,1},{6,2},{7,3},{8,12},{9,13},{10,... | collective-permute-start | bytes 98312 | tf_op jit(solution)/shard_map/ppermute | solution.py:646
  34.7 5.3 %collective-permute-start.7 = (f32[6,32,128]{2,1,0:T(8,128)S(1)}, f32[6,32,128]{2,1,0:T(8,128)S(1)}, u32[]{:S(2)}, u32[]{:S(2)}) collective-permute-start(f32[6,32,128]{2,1,0:T(8,128)S(1)} %sent_modes.1), channel_id=1, source_target_pairs={{0,1},{1,0},{2,3},{3,2},{4,5},{5,4},{6,7},{7,6},{8,9},{9,8},{10,11... | collective-permute-start | bytes 294920 | tf_op jit(solution)/shard_map/ppermute | solution.py:646
  37.4 1.3 %collective-permute-start.6 = (f32[128,128]{1,0:T(8,128)S(1)}, f32[128,128]{1,0:T(8,128)S(1)}, u32[]{:S(2)}, u32[]{:S(2)}) collective-permute-start(f32[128,128]{1,0:T(8,128)S(1)} %join_y.1.refs_0_), channel_id=1, source_target_pairs={{0,2},{1,3},{2,0},{3,1},{4,6},{5,7},{6,4},{7,5},{8,10},{9,11},{10,... | collective-permute-start | bytes 196616 | tf_op jit(solution)/shard_map/ppermute | solution.py:646
